TPU v7x, 128 devices: a whole 4x4x4 slice. The times are simulated.
128 devices in a mesh: island: 2 (over y_lo), fsdp: 64 (over y_hi, z, x, core).
Axes of the slice: x: 4, y: 4 (y_hi: 2, y_lo: 2; y = y_hi * 2 + y_lo), z: 4, core: 2. Of those that a mesh axis runs over, the one named last changes fastest.
Arguments:
- tokens: bfloat16 [2, 1024, 8192], P('island', 'fsdp'), may hold values from -6 to 6
- hidden_grad: bfloat16 [2, 1024, 16384], P('island', None, 'fsdp'), may hold values from -1.5 to 1.5
- gate_weight: bfloat16 [2, 8192, 16384], P('island', None, 'fsdp'), as said below
- up_weight: bfloat16 [2, 8192, 16384], P('island', None, 'fsdp'), as said below
- momentum: bfloat16 [2, 8192, 16384], P(None, ('island', 'fsdp')), may hold values from -6 to 6
- layouts: int32 [2, 128], replicated, may hold values from 0 to 127, as said below
Outputs:
- gate_update: bfloat16 [2, 8192, 16384], P('island', None, 'fsdp')
- up_update: bfloat16 [2, 8192, 16384], P('island', None, 'fsdp')
- new_momentum: bfloat16 [2, 8192, 16384], P(None, ('island', 'fsdp'))
Inputs may be any that keep to these rules, and one draw needn't show every extreme that they name: Each row of layouts orders all 128 blocks. Device j of fsdp in island i holds blocks layouts[i, j * 2] to layouts[i, (j + 1) * 2 - 1], in that order, as its columns of gate_weight, up_weight, hidden_grad and the updates. gate_weight[i] is the same matrix for every island i, its column blocks in island i's order. up_weight[i] is the same matrix for every island i, its column blocks in island i's order.
All inputs are finite; a program needn't handle non-finite values.
Results may differ from a plain program's by a relative error of at most 0.011.
Values may be sent and summed in bfloat16 or wider, within the bound.
A program may use at most 128 MiB of HBM per device.

v0:
```python
import jax
import jax.numpy as jnp
from jax import lax
from jax.sharding import PartitionSpec as P

FFW = 16384
BLOCK = 128


inner_rate = 0.25
outer_rate = 0.7
momentum_decay = 0.9


def cotangents(gate_pre, up_pre, upstream):
    logistic = jax.nn.sigmoid(gate_pre)
    upstream_wide = upstream.astype(jnp.float32)
    d_gate = (upstream_wide * up_pre * logistic * (1.0 + gate_pre * (1.0 - logistic))).astype(
        jnp.bfloat16
    )
    d_up = (upstream_wide * gate_pre * logistic).astype(jnp.bfloat16)
    return (d_gate, d_up)


def shards(tokens, hidden_grad, gate_weight, up_weight, momentum, layouts):
    contract = (((0,), (0,)), ((), ()))
    w_gate = gate_weight[0]
    w_up = up_weight[0]
    upstream = hidden_grad[0]
    own_rows = tokens[0]
    model_width = w_gate.shape[0]
    local_width = w_gate.shape[1]
    gathered = lax.all_gather(own_rows, "fsdp", axis=0, tiled=True)
    gate_pre = jnp.dot(gathered, w_gate, preferred_element_type=jnp.float32)
    up_pre = jnp.dot(gathered, w_up, preferred_element_type=jnp.float32)
    d_gate, d_up = cotangents(gate_pre, up_pre, upstream)
    grad_gate = lax.dot_general(gathered, d_gate, contract, preferred_element_type=jnp.float32)
    grad_up = lax.dot_general(gathered, d_up, contract, preferred_element_type=jnp.float32)
    pseudo = jnp.stack(
        [(inner_rate * grad_gate).astype(jnp.bfloat16), (inner_rate * grad_up).astype(jnp.bfloat16)]
    )
    islands = lax.axis_size("island")
    members = lax.axis_size("fsdp")
    peers = islands * members
    block_count = layouts.shape[1]
    slab = model_width // peers
    blocks_here = local_width // BLOCK
    outgoing = pseudo.reshape(2, peers, slab, local_width)
    received = lax.all_to_all(outgoing, ("island", "fsdp"), split_axis=1, concat_axis=1, tiled=True)
    arranged = jnp.transpose(received.reshape(2, peers, slab, blocks_here, BLOCK), (0, 2, 1, 3, 4))
    arranged = arranged.reshape(2, slab, islands * block_count, BLOCK)
    shifts = (jnp.arange(islands, dtype=jnp.int32) * block_count)[:, None]
    inverse = (jnp.argsort(layouts, axis=1) + shifts).reshape(-1)
    picked = jnp.take(arranged, inverse, axis=2).reshape(2, slab, islands, FFW)
    summed = jnp.sum(picked.astype(jnp.float32), axis=2)
    average = summed / islands
    state = momentum_decay * momentum.astype(jnp.float32) + average
    update = (outer_rate * (average + momentum_decay * state)).astype(jnp.bfloat16)
    arranged_update = update.reshape(2, slab, block_count, BLOCK)
    placed = jnp.take(arranged_update, layouts.reshape(-1), axis=2).reshape(
        2, slab, peers, local_width
    )
    placed = jnp.transpose(placed, (0, 2, 1, 3))
    returned = lax.all_to_all(placed, ("island", "fsdp"), split_axis=1, concat_axis=1, tiled=True)
    returned = returned.reshape(2, model_width, local_width)
    return (returned[0][None], returned[1][None], state.astype(jnp.bfloat16))


def solution(mesh):
    placed = (
        P("island", "fsdp", None),
        P("island", None, "fsdp"),
        P("island", None, "fsdp"),
        P("island", None, "fsdp"),
        P(None, ("island", "fsdp"), None),
        P(),
    )
    return jax.shard_map(
        shards,
        mesh=mesh,
        in_specs=placed,
        out_specs=(
            P("island", None, "fsdp"),
            P("island", None, "fsdp"),
            P(None, ("island", "fsdp"), None),
        ),
        check_vma=False,
    )
```

profile of v0, /device:TPU:7, one launch (start us, length us, event | category | flops | bytes accessed | tf_op | source)
XLA Modules:
  0.0 599.2 jit_solution(6096164828761469376)
XLA Ops:
  8.0 0.7 all-gather.3.cloned.1.call-update
  8.7 112.2 %all-gather.3.cloned.1.call-done = bf16[1,1024,8192]{2,1,0:T(8,128)(2,1)} async-done(((bf16[1,16,8192]{2,1,0:T(8,128)(2,1)}), bf16[1,1024,8192]{2,1,0:T(8,128)(2,1)}) %all-gather.3.cloned.1.call-update) | async-done | bytes 16777232 | tf_op jit(solution)/shard_map/all_gather | solution.py:33
  120.9 9.3 %fusion.4 = f32[1024,256]{1,0:T(8,128)S(1)} fusion(bf16[1,1024,8192]{2,1,0:T(8,128)(2,1)} %all-gather.3.cloned.1.call-done, bf16[1,8192,256]{2,1,0:T(8,128)(2,1)} %param.8), kind=kOutput, calls=%fused_computation.6 | convolution fusion | flops 4294967296 | bytes 22020096 | tf_op jit(solution)/shard_map/dot_general | solution.py:34
  130.2 31.6 %fusion.20 = bf16[8192,256]{0,1:T(8,128)(2,1)} fusion(bf16[1,1024,8192]{2,1,0:T(8,128)(2,1)} %all-gather.3.cloned.1.call-done, bf16[1,8192,256]{2,1,0:T(8,128)(2,1)} %param.9, f32[1024,256]{1,0:T(8,128)S(1)} %fusion.4, bf16[1,1024,256]{2,1,0:T(8,128)(2,1)S(1)} %copy-done.2), kind=kOutput, calls=%fused_computation.16 | convolution fusion | flops 8597012480 | bytes 26738688 | tf_op jit(solution)/shard_map/dot_general | solution.py:37
  161.8 6.4 %copy.46 = bf16[8192,256]{1,0:T(8,128)(2,1)} copy(bf16[8192,256]{0,1:T(8,128)(2,1)} %fusion.20) | data formatting | bytes 8388608 | tf_op jit(solution)/shard_map/convert_element_type | solution.py:40
  168.2 12.4 %fusion.23 = bf16[8192,256]{0,1:T(8,128)(2,1)} fusion(bf16[1,1024,8192]{2,1,0:T(8,128)(2,1)} %all-gather.3.cloned.1.call-done, f32[1024,256]{1,0:T(8,128)S(1)} %fusion.4, bf16[1,1024,256]{2,1,0:T(8,128)(2,1)S(1)} %copy-done.2), kind=kOutput, calls=%fused_computation.17 | convolution fusion | flops 4300996608 | bytes 22544384 | tf_op jit(solution)/shard_map/dot_general | solution.py:38
  180.6 6.4 %copy.47 = bf16[8192,256]{1,0:T(8,128)(2,1)} copy(bf16[8192,256]{0,1:T(8,128)(2,1)} %fusion.23) | data formatting | bytes 8388608 | tf_op jit(solution)/shard_map/convert_element_type | solution.py:40
  186.9 7.5 %pad_maximum_fusion = bf16[2,128,64,256]{3,2,1,0:T(8,128)(2,1)} fusion(bf16[1,128,64,256]{3,2,1,0:T(8,128)(2,1)} %bitcast.102, bf16[1,128,64,256]{3,2,1,0:T(8,128)(2,1)} %bitcast.101), kind=kLoop, calls=%fused_computation.18 | loop fusion | flops 4194304 | bytes 16777216 | tf_op jit(solution)/shard_map/stack | solution.py:39
  194.4 8.3 %copy.48 = bf16[2,128,64,256]{3,2,0,1:T(8,128)(2,1)} copy(bf16[2,128,64,256]{3,2,1,0:T(8,128)(2,1)} %pad_maximum_fusion) | data formatting | bytes 16777216 | tf_op jit(solution)/shard_map/stack | solution.py:39
  202.7 6.1 %all-to-all-start = ((bf16[2,128,64,256]{3,2,0,1:T(8,128)(2,1)}), bf16[2,128,64,256]{3,2,0,1:T(8,128)(2,1)}, u32[]{:S(2)}, u32[]{:S(2)}) async-start(bf16[2,128,64,256]{3,2,0,1:T(8,128)(2,1)} %copy.48), calls=%async_computation | async-start | bytes 16777216 | tf_op jit(solution)/shard_map/all_to_all | solution.py:49
  208.8 0.6 iota.12
  209.4 0.1 reshape.116
  209.8 0.1 copy.45
  209.9 4.6 sort.19.cloned.1.call-done
  214.5 0.8 compare_and_fusion.1
  215.3 0.1 broadcast_bitcast_fusion
  215.5 103.9 %all-to-all-done = bf16[2,128,64,256]{3,2,0,1:T(8,128)(2,1)} async-done(((bf16[2,128,64,256]{3,2,0,1:T(8,128)(2,1)}), bf16[2,128,64,256]{3,2,0,1:T(8,128)(2,1)}, u32[]{:S(2)}, u32[]{:S(2)}) %all-to-all-start) | async-done | bytes 8388640 | tf_op jit(solution)/shard_map/all_to_all | solution.py:49
  319.4 12.8 %copy.49 = bf16[2,128,64,256]{1,3,2,0:T(8,128)(2,1)} copy(bf16[2,128,64,256]{3,2,0,1:T(8,128)(2,1)} %all-to-all-done) | data formatting | bytes 16777216 | tf_op jit(solution)/shard_map/all_to_all | solution.py:49
  332.2 12.0 %copy.50 = bf16[2,64,128,2,128]{4,1,3,2,0:T(8,128)(2,1)} copy(bf16[2,64,128,2,128]{2,4,3,1,0:T(8,128)(2,1)} %bitcast.100) | data formatting | bytes 16777216 | tf_op jit(solution)/shard_map/transpose | solution.py:50
  344.2 12.0 %gather_fusion = bf16[256,2,64,128]{3,2,1,0:T(8,128)(2,1)} fusion(bf16[2,64,256,128]{3,1,2,0:T(8,128)(2,1)} %bitcast.97, s32[1024]{0:T(1024)S(1)} %pad_clamp_fusion.1), kind=kCustom, calls=%fused_computation | custom fusion | bytes 16778240 | tf_op jit(solution)/shard_map/jit(_take)/gather | solution.py:54
  356.2 12.0 %copy.51 = bf16[2,64,256,128]{3,2,1,0:T(8,128)(2,1)} copy(bf16[2,64,256,128]{3,1,0,2:T(8,128)(2,1)} %bitcast.98) | data formatting | bytes 16777216 | tf_op jit(solution)/shard_map/jit(_take)/gather | solution.py:54
  368.2 12.5 %gather.13 = bf16[2,64,2,16384]{3,2,1,0:T(2,128)(2,1)} reshape(bf16[2,64,256,128]{3,2,1,0:T(8,128)(2,1)} %copy.51) | data formatting | bytes 16777216 | tf_op jit(solution)/shard_map/jit(_take)/gather | solution.py:54
  380.7 27.8 %convert_reduce_fusion = f32[2,64,16384]{2,1,0:T(8,128)} fusion(bf16[2,64,2,16384]{3,2,1,0:T(2,128)(2,1)} %gather.13, pred[2,16384]{1,0:T(4,128)(4,1)S(1)} %bitcast.105), kind=kLoop, calls=%fused_computation.10 | loop fusion | flops 10485760 | bytes 16809984 | tf_op jit(solution)/shard_map/reduce_sum | solution.py:55
  408.5 6.1 %fusion.26 = (bf16[2,64,16384]{2,1,0:T(8,128)(2,1)}, bf16[2,8,128,8,128]{4,3,2,1,0:T(8,128)(2,1)S(1)}) fusion(bf16[2,64,16384]{2,1,0:T(8,128)(2,1)S(1)} %copy-done, f32[2,64,16384]{2,1,0:T(8,128)} %convert_reduce_fusion), kind=kLoop, calls=%fused_computation.22 | loop fusion | flops 18874368 | bytes 20971520 | tf_op jit(solution)/shard_map/convert_element_type | solution.py:66
  414.7 3.2 copy.63
  417.9 10.8 %gather_fusion.1 = bf16[256,2,64,128]{3,2,1,0:T(8,128)(2,1)} fusion(bf16[2,64,128,128]{3,1,2,0:T(8,128)(2,1)} %bitcast.96, s32[1024]{0:T(1024)S(1)} %pad_clamp_fusion), kind=kCustom, calls=%fused_computation.1 | custom fusion | bytes 16778240 | tf_op jit(solution)/shard_map/jit(_take)/gather | solution.py:60
  428.7 12.0 %copy.53 = bf16[2,64,256,128]{3,2,1,0:T(8,128)(2,1)} copy(bf16[2,64,256,128]{3,1,0,2:T(8,128)(2,1)} %bitcast.99) | data formatting | bytes 16777216 | tf_op jit(solution)/shard_map/jit(_take)/gather | solution.py:60
  440.7 13.1 %gather.15 = bf16[2,64,128,256]{3,2,1,0:T(8,128)(2,1)} reshape(bf16[2,64,256,128]{3,2,1,0:T(8,128)(2,1)} %copy.53) | data formatting | bytes 16777216 | tf_op jit(solution)/shard_map/jit(_take)/gather | solution.py:60
  453.8 7.4 %select_bitcast_fusion = bf16[2,128,64,256]{3,1,2,0:T(8,128)(2,1)} fusion(bf16[2,64,128,256]{3,2,1,0:T(8,128)(2,1)} %gather.15, pred[128,256]{1,0:T(8,128)(4,1)S(1)} %copy.45), kind=kLoop, calls=%fused_computation.19 | loop fusion | flops 4194304 | bytes 16809984 | tf_op jit(solution)/shard_map/transpose | solution.py:63
  461.3 11.4 %copy.54 = bf16[2,128,64,256]{3,2,0,1:T(8,128)(2,1)} copy(bf16[2,128,64,256]{3,1,2,0:T(8,128)(2,1)} %select_bitcast_fusion) | data formatting | bytes 16777216 | tf_op jit(solution)/shard_map/transpose | solution.py:63
  472.6 115.0 %all_to_all.10 = bf16[2,128,64,256]{3,2,0,1:T(8,128)(2,1)S(1)} all-to-all(bf16[2,128,64,256]{3,2,0,1:T(8,128)(2,1)} %copy.54), channel_id=1, replica_groups=mesh['island'=2,'fsdp'=64] {'island','fsdp'}, dimensions={1} | all-to-all | bytes 16777216 | tf_op jit(solution)/shard_map/all_to_all | solution.py:64
  587.6 3.9 fusion.66
  (18 shorter events, 0.3 us)
Async XLA Ops:
  8.0 112.9 %all-gather.3.cloned.1.call-start = ((), (), s32[]{:S(2)}) async-start(), calls=%async_computation.2 | async-start | bytes 17039360 | tf_op jit(solution)/shard_map/all_gather | solution.py:33
  8.7 121.5 %copy-start.2 = (bf16[1,1024,256]{2,1,0:T(8,128)(2,1)S(1)}, bf16[1,1024,256]{2,1,0:T(8,128)(2,1)}, u32[]{:S(2)}) copy-start(bf16[1,1024,256]{2,1,0:T(8,128)(2,1)} %param.7) | copy-start | bytes 1572868
  202.7 6.8 %copy-start.1 = (s32[2,128]{1,0:T(2,128)S(1)}, s32[2,128]{1,0:T(2,128)}, u32[]{:S(2)}) copy-start(s32[2,128]{1,0:T(2,128)} %param.11) | copy-start | bytes 3076
  202.7 116.7 %all-to-all-start = ((bf16[2,128,64,256]{3,2,0,1:T(8,128)(2,1)}), bf16[2,128,64,256]{3,2,0,1:T(8,128)(2,1)}, u32[]{:S(2)}, u32[]{:S(2)}) async-start(bf16[2,128,64,256]{3,2,0,1:T(8,128)(2,1)} %copy.48), calls=%async_computation | async-start | bytes 16777216 | tf_op jit(solution)/shard_map/all_to_all | solution.py:49
  208.8 5.7 sort.19.cloned.1.call-start
  380.7 27.8 %copy-start = (bf16[2,64,16384]{2,1,0:T(8,128)(2,1)S(1)}, bf16[2,64,16384]{2,1,0:T(8,128)(2,1)}, u32[]{:S(2)}) copy-start(bf16[2,64,16384]{2,1,0:T(8,128)(2,1)} %param.10) | copy-start | bytes 12582916
Sparse Core Ops, SparseCore 0:
  12.0 108.8 all-gather.2
Sparse Core Ops, SparseCore 1:
  212.1 2.2 sort.21.cloned.1.call-done
  (1 shorter events, 0.0 us)
where the time goes:
time: 611 us; the launch traced here: 599 us
  waiting for transfers between devices  217 us (36%)
  local copies, waits for them, and re-layouts  143 us (23%)
  blocking collectives  115 us (19%)
  matrix products  53.3 us (9%)
  other arithmetic  49.7 us (8%)
  between operations  15.8 us (3%)
  starting transfers between devices  6.15 us (1%)
    all_to_all x1, blocking collectives, shards(): lax.all_to_all(placed, ('island', 'fsdp'), split_axis=1, concat_axis=1, t...  115 us
    all_gather x1, waiting for transfers between devices, shards(): gathered = lax.all_gather(own_rows, 'fsdp', axis=0, tiled=True)  112 us
    all_to_all x1, waiting for transfers between devices, shards(): lax.all_to_all(outgoing, ('island', 'fsdp'), split_axis=1, concat_axis=1,...  104 us
    gather x3, local copies, waits for them, and re-layouts, shards(): picked = jnp.take(arranged, inverse, axis=2).reshape(2, slab, islands, FFW)  36.5 us
    gather x3, local copies, waits for them, and re-layouts, shards(): jnp.take(arranged_update, layouts.reshape(-1), axis=2)  35.9 us
    dot_general x1, matrix products, shards(): lax.dot_general(gathered, d_gate, contract, preferred_element_type=jnp.fl...  31.6 us
    reduce_sum x1, other arithmetic, shards(): summed = jnp.sum(picked.astype(jnp.float32), axis=2)  27.8 us
    all_to_all x1, local copies, waits for them, and re-layouts, shards(): lax.all_to_all(outgoing, ('island', 'fsdp'), split_axis=1, concat_axis=1,...  12.8 us
  transfers between devices with their start and end apart: 2, of which 2 were waited for; matrix products, arithmetic and copies ran while one was open for 0% of the time, Pallas kernels for 0%

commit v1 on v0

v1 whole, which is shorter than its diff:
```python
import jax
import jax.numpy as jnp
from jax import lax
from jax.experimental import pallas as pl
from jax.experimental.pallas import tpu as pltpu
from jax.sharding import PartitionSpec as P

BLOCK = 128
BY_MESH = pl.DeviceIdType.MESH

inner_rate = 0.25
outer_rate = 0.7
momentum_decay = 0.9

ISLANDS = 2
MEMBERS = 64
PEERS = ISLANDS * MEMBERS
CHIPS = PEERS // 2
ROWS = 64
OWN_TOKENS = 16
STRIDE = 91


def position():
    island = lax.axis_index("island")
    member = lax.axis_index("fsdp")
    return (member // 32) * 2 + island, (member // 8) % 4, (member // 2) % 4, member % 2


def member_of(y, z, x, core):
    return (y // 2) * 32 + z * 8 + x * 2 + core


def slot(far, sibling, near, half):
    return ((far * 2 + sibling) * 4 + near) * 2 + half


def cotangents(gate_pre, up_pre, upstream):
    logistic = jax.nn.sigmoid(gate_pre)
    d_gate = upstream * up_pre * logistic * (1.0 + gate_pre * (1.0 - logistic))
    d_up = upstream * gate_pre * logistic
    return d_gate.astype(jnp.bfloat16), d_up.astype(jnp.bfloat16)


def kernel(
    tokens_ref,
    hidden_ref,
    gate_ref,
    up_ref,
    momentum_ref,
    layout_ref,
    inverse_ref,
    gate_out,
    up_out,
    momentum_out,
    tokens,
    weights,
    hidden,
    cotangent,
    outgoing,
    received,
    momentum,
    update,
    gate_sum,
    up_sum,
    load_sem,
    hidden_sem,
    tokens_sem,
    gather_sent,
    gather_got,
    sums_sent,
    sums_got,
    own_sem,
    updates_sent,
    gate_got,
    up_got,
):
    y, z, x, core = position()
    island = lax.axis_index("island")
    member = lax.axis_index("fsdp")
    me = island * MEMBERS + member

    def partner(step):
        dy, dz, dx, dc = step // 32, (step // 8) % 4, (step // 2) % 4, step % 2
        there_y = (y + dy) % 4
        there = member_of(there_y, (z + dz) % 4, (x + dx) % 4, (core + dc) % 2)
        return there_y % 2, there

    barrier = pltpu.get_barrier_semaphore()

    def greet(step, carry):
        pl.semaphore_signal(barrier, inc=1, device_id=partner(step), device_id_type=BY_MESH)
        return carry

    lax.fori_loop(1, PEERS, greet, 0)

    loads = [
        pltpu.make_async_copy(gate_ref, weights.at[0], load_sem.at[0]),
        pltpu.make_async_copy(up_ref, weights.at[1], load_sem.at[1]),
        pltpu.make_async_copy(momentum_ref, momentum, load_sem.at[2]),
    ]
    own_tokens = pltpu.make_async_copy(tokens_ref, tokens.at[0], tokens_sem)
    own_tokens.start()

    def load_hidden(place, carry):
        half, near, sibling, far = place % 2, (place // 2) % 4, (place // 8) % 2, place // 16
        their_core = (core + sibling) % 2
        dx = near * (1 - their_core) + far * their_core
        dz = near * their_core + far * (1 - their_core)
        there = member_of((y + 2 * half) % 4, (z + dz) % 4, (x + dx) % 4, their_core)
        rows = pl.ds(pl.multiple_of(there * OWN_TOKENS, OWN_TOKENS), OWN_TOKENS)
        pltpu.make_async_copy(hidden_ref.at[rows], hidden.at[place], hidden_sem).start()
        return carry

    lax.fori_loop(0, MEMBERS, load_hidden, 0)
    for load in loads:
        load.start()

    pl.semaphore_wait(barrier, PEERS - 1)

    def along_near(sign):
        return member_of(y, (z + sign * core + 4) % 4, (x + sign * (1 - core) + 4) % 4, core)

    def along_far(sign):
        return member_of(y, (z + sign * (1 - core) + 4) % 4, (x + sign * core + 4) % 4, core)

    other_plane = member_of((y + 2) % 4, z, x, core)
    other_core = member_of(y, z, x, 1 - core)

    def send_tokens(source, place, to):
        pltpu.make_async_remote_copy(
            src_ref=source,
            dst_ref=tokens.at[place],
            send_sem=gather_sent,
            recv_sem=gather_got.at[place],
            device_id=(island, to),
            device_id_type=BY_MESH,
        ).start()

    def arrived(place):
        pltpu.make_async_copy(tokens.at[place], tokens.at[place], gather_got.at[place]).wait()

    def spread(source, near, half):
        send_tokens(source, slot(3, 0, near, half), along_far(1))
        send_tokens(source, slot(1, 0, near, half), along_far(-1))
        send_tokens(source, slot(0, 1, near, half), other_core)

    def ring(source, half):
        send_tokens(source, slot(0, 0, 3, half), along_near(1))
        send_tokens(source, slot(0, 0, 1, half), along_near(-1))

    send_tokens(tokens_ref, slot(0, 0, 0, 1), other_plane)
    ring(tokens_ref, 0)
    spread(tokens_ref, 0, 0)

    place = slot(0, 0, 0, 1)
    arrived(place)
    ring(tokens.at[place], 1)
    spread(tokens.at[place], 0, 1)
    for half in range(2):
        before, after = slot(0, 0, 3, half), slot(0, 0, 1, half)
        arrived(before)
        if half == 0:
            send_tokens(tokens.at[before], slot(0, 0, 2, 0), along_near(1))
        arrived(after)
        if half == 1:
            send_tokens(tokens.at[after], slot(0, 0, 2, 1), along_near(-1))
        spread(tokens.at[before], 3, half)
        spread(tokens.at[after], 1, half)
    for half in range(2):
        place = slot(0, 0, 2, half)
        arrived(place)
        spread(tokens.at[place], 2, half)

    def forward(far):
        depth = 1024
        for part in range(8):
            cols = pl.ds(part * depth, depth)
            rows = tokens[pl.ds(far * 16, 16), :, cols].reshape(256, depth)
            gate_part = jnp.dot(rows, weights[0, cols, :], preferred_element_type=jnp.float32)
            up_part = jnp.dot(rows, weights[1, cols, :], preferred_element_type=jnp.float32)
            if part == 0:
                gate_sum[...] = gate_part
                up_sum[...] = up_part
            else:
                gate_sum[...] += gate_part
                up_sum[...] += up_part
        upstream = hidden[pl.ds(far * 16, 16)].reshape(256, 256).astype(jnp.float32)
        d_gate, d_up = cotangents(gate_sum[...], up_sum[...], upstream)
        cotangent[pl.ds(far * 256, 256), 0:256] = d_gate
        cotangent[pl.ds(far * 256, 256), 256:512] = d_up

    own_tokens.wait()
    loads[0].wait()
    loads[1].wait()
    pltpu.make_async_copy(hidden, hidden, hidden_sem).wait()
    for near in range(4):
        for half in range(2):
            arrived(slot(0, 1, near, half))
    forward(0)

    order = [(0, 0), (0, 1), (1, 0), (3, 0), (1, 1), (3, 1), (2, 0), (2, 1)]
    for near, half in order:
        before, after = slot(3, 0, near, half), slot(1, 0, near, half)
        arrived(before)
        if half == 0:
            send_tokens(tokens.at[before], slot(2, 0, near, 0), along_far(1))
        send_tokens(tokens.at[before], slot(3, 1, near, half), other_core)
        arrived(after)
        if half == 1:
            send_tokens(tokens.at[after], slot(2, 0, near, 1), along_far(-1))
        send_tokens(tokens.at[after], slot(1, 1, near, half), other_core)
    for far in (3, 1):
        for near, half in order:
            arrived(slot(far, 1, near, half))
        forward(far)
    for near, half in order:
        place = slot(2, 0, near, half)
        arrived(place)
        send_tokens(tokens.at[place], slot(2, 1, near, half), other_core)
    for near, half in order:
        arrived(slot(2, 1, near, half))
    forward(2)

    def backward(group, carry):
        steps = [((group * 4 + k) * STRIDE) % CHIPS for k in range(4)]
        chips = []
        for step in steps:
            there_island, there = partner(step * 2)
            chips.append(there_island * 32 + there // 2)
        columns = [
            tokens[:, :, pl.ds(pl.multiple_of(chip * BLOCK, BLOCK), BLOCK)].reshape(1024, BLOCK)
            for chip in chips
        ]
        summed = lax.dot_general(
            jnp.concatenate(columns, axis=1),
            cotangent[...],
            (((0,), (0,)), ((), ())),
            preferred_element_type=jnp.float32,
        )
        scaled = (inner_rate * summed).astype(jnp.bfloat16)
        for k in range(4):
            for half in range(2):
                first = k * BLOCK + half * ROWS
                for part in range(4):
                    matrix, block = part // 2, part % 2
                    outgoing[(chips[k] * 2 + half) * 2 + block, matrix] = scaled[
                        first : first + ROWS, part * BLOCK : (part + 1) * BLOCK
                    ]
        for k in range(4):
            for dc in range(2):
                there_island, there = partner(steps[k] * 2 + dc)
                number = there_island * MEMBERS + there

                @pl.when(number != me)
                def _():
                    pltpu.make_async_remote_copy(
                        src_ref=outgoing.at[pl.ds(number * 2, 2)],
                        dst_ref=received.at[pl.ds(me * 2, 2)],
                        send_sem=sums_sent,
                        recv_sem=sums_got,
                        device_id=(there_island, there),
                        device_id_type=BY_MESH,
                    ).start()

        return carry

    lax.fori_loop(0, CHIPS // 4, backward, 0)
    received[pl.ds(me * 2, 2)] = outgoing[pl.ds(me * 2, 2)]
    loads[2].wait()
    others = received.at[pl.ds(0, (PEERS - 1) * 2)]
    pltpu.make_async_copy(others, others, sums_got).wait()

    def outer_step(block, carry):
        first = inverse_ref[0, block]
        second = inverse_ref[1, block]
        cols = pl.ds(pl.multiple_of(block * BLOCK, BLOCK), BLOCK)
        for matrix in range(2):
            one = received[first, matrix].astype(jnp.float32)
            two = received[second, matrix].astype(jnp.float32)
            average = (one + two) * (1.0 / ISLANDS)
            state = momentum_decay * momentum[matrix, :, cols].astype(jnp.float32) + average
            momentum[matrix, :, cols] = state.astype(jnp.bfloat16)
            update[block, matrix] = (outer_rate * (average + momentum_decay * state)).astype(
                jnp.bfloat16
            )
        return carry

    lax.fori_loop(0, PEERS, outer_step, 0)
    keep = pltpu.make_async_copy(momentum, momentum_out, load_sem.at[2])
    keep.start()

    mine = pl.ds(pl.multiple_of(me * ROWS, ROWS), ROWS)

    def stage(number, there_island, there):
        rows = pl.ds(pl.multiple_of(number * ROWS, ROWS), ROWS)
        for half in range(2):
            block = layout_ref[there_island, there * 2 + half]
            for matrix in range(2):
                weights[matrix, rows, half * BLOCK : (half + 1) * BLOCK] = update[block, matrix]
        return rows

    def give_back(index, carry):
        step = (index * STRIDE) % PEERS
        there_island, there = partner(step)
        rows = stage(there_island * MEMBERS + there, there_island, there)
        for matrix, (out, got) in enumerate(((gate_out, gate_got), (up_out, up_got))):
            pltpu.make_async_remote_copy(
                src_ref=weights.at[matrix, rows],
                dst_ref=out.at[mine],
                send_sem=updates_sent,
                recv_sem=got,
                device_id=(there_island, there),
                device_id_type=BY_MESH,
            ).start()
        return carry

    lax.fori_loop(1, PEERS, give_back, 0)
    stage(me, island, member)
    own = [
        pltpu.make_async_copy(weights.at[0, mine], gate_out.at[mine], own_sem.at[0]),
        pltpu.make_async_copy(weights.at[1, mine], up_out.at[mine], own_sem.at[1]),
    ]
    for copy in own:
        copy.start()
    for copy in own:
        copy.wait()
    keep.wait()
    sent = tokens.at[pl.ds(0, 63)]
    pltpu.make_async_copy(sent, sent, gather_sent).wait()
    pltpu.make_async_copy(others, others, sums_sent).wait()
    for out, got in ((gate_out, gate_got), (up_out, up_got)):
        part = out.at[pl.ds(0, (PEERS - 1) * ROWS)]
        pltpu.make_async_copy(part, part, got).wait()
    pltpu.make_async_copy(others, others, updates_sent).wait()


def shards(tokens, hidden_grad, gate_weight, up_weight, momentum, layouts):
    blocks = layouts.shape[1]
    places = jnp.arange(blocks, dtype=jnp.int32)
    hit = layouts[:, :, None] == places[None, None, :]
    inverse = jnp.sum(jnp.where(hit, places[None, :, None], 0), axis=1, dtype=jnp.int32)
    inverse = inverse + jnp.arange(ISLANDS, dtype=jnp.int32)[:, None] * blocks
    anywhere = pl.BlockSpec(memory_space=pl.ANY)
    scalars = pl.BlockSpec(memory_space=pltpu.SMEM)
    bf16 = jnp.bfloat16
    gate, up, state = pl.pallas_call(
        kernel,
        out_shape=(
            jax.ShapeDtypeStruct((8192, 256), bf16),
            jax.ShapeDtypeStruct((8192, 256), bf16),
            jax.ShapeDtypeStruct((2, ROWS, 16384), bf16),
        ),
        in_specs=[anywhere] * 5 + [scalars] * 2,
        out_specs=(anywhere, anywhere, anywhere),
        scratch_shapes=[
            pltpu.VMEM((MEMBERS, OWN_TOKENS, 8192), bf16),
            pltpu.VMEM((2, 8192, 256), bf16),
            pltpu.VMEM((MEMBERS, OWN_TOKENS, 256), bf16),
            pltpu.VMEM((1024, 512), bf16),
            pltpu.VMEM((PEERS * 2, 2, ROWS, BLOCK), bf16),
            pltpu.VMEM((PEERS * 2, 2, ROWS, BLOCK), bf16),
            pltpu.VMEM((2, ROWS, 16384), bf16),
            pltpu.VMEM((PEERS, 2, ROWS, BLOCK), bf16),
            pltpu.VMEM((256, 256), jnp.float32),
            pltpu.VMEM((256, 256), jnp.float32),
            pltpu.SemaphoreType.DMA((3,)),
            pltpu.SemaphoreType.DMA,
            pltpu.SemaphoreType.DMA,
            pltpu.SemaphoreType.DMA,
            pltpu.SemaphoreType.DMA((64,)),
            pltpu.SemaphoreType.DMA,
            pltpu.SemaphoreType.DMA,
            pltpu.SemaphoreType.DMA((2,)),
            pltpu.SemaphoreType.DMA,
            pltpu.SemaphoreType.DMA,
            pltpu.SemaphoreType.DMA,
        ],
        compiler_params=pltpu.CompilerParams(
            collective_id=0, has_side_effects=True, vmem_limit_bytes=62 * 2**20
        ),
    )(tokens[0], hidden_grad[0], gate_weight[0], up_weight[0], momentum, layouts, inverse)
    return gate[None], up[None], state


def solution(mesh):
    placed = (
        P("island", "fsdp", None),
        P("island", None, "fsdp"),
        P("island", None, "fsdp"),
        P("island", None, "fsdp"),
        P(None, ("island", "fsdp"), None),
        P(),
    )
    return jax.shard_map(
        shards,
        mesh=mesh,
        in_specs=placed,
        out_specs=(
            P("island", None, "fsdp"),
            P("island", None, "fsdp"),
            P(None, ("island", "fsdp"), None),
        ),
        check_vma=False,
    )
```

time: 611 us -> 324 us (0.53)
  the two profiles are of different devices: /device:TPU:7 before, /device:TPU:4 now
where the time goes in v1:
time: 324 us
  Pallas kernels  312 us (96%)
  local copies, waits for them, and re-layouts  10.3 us (3%)
    pallas_call x1, Pallas kernels, shards(): pl.pallas_call(kernel, out_shape=(jax.ShapeDtypeStruct((8192, 256), bf16)...  312 us
    unnamed x7, local copies, waits for them, and re-layouts  10.3 us

profile of v1, /device:TPU:4, one launch (start us, length us, event | category | flops | bytes accessed | tf_op | source)
XLA Modules:
  0.0 324.1 jit_solution(7415241964206701409)
XLA Ops:
  0.6 0.8 select_reduce_fusion
  1.4 0.6 broadcast_add_fusion.inverse_ref
  2.1 311.7 %shard_map.85 = (bf16[8192,256]{1,0:T(8,128)(2,1)}, bf16[8192,256]{1,0:T(8,128)(2,1)}, bf16[2,64,16384]{2,1,0:T(8,128)(2,1)}) custom-call(bf16[16,8192]{1,0:T(8,128)(2,1)} %bitcast.11, bf16[1024,256]{1,0:T(8,128)(2,1)} %bitcast.10, bf16[8192,256]{1,0:T(8,128)(2,1)} %bitcast.6, bf16[8192,256]{1,0:T(8,128)(2,1)} %bitcast.7, ...), custom_call_target="tpu_custom_call" | custom-call | tf_op jit(solution)/shard_map/pallas_call | solution.py:347
  313.8 0.0 copy-start.1
  313.8 4.6 %copy.12 = bf16[1,8192,256]{2,1,0:T(8,128)(2,1)} copy(bf16[1,8192,256]{2,1,0:T(8,128)(2,1)} %bitcast.9) | data formatting | bytes 8388608
  318.4 0.0 copy-done.1
  318.4 0.0 copy-start
  318.4 2.1 copy.13
  320.5 1.6 copy-done
  322.1 2.0 copy.14
  (1 shorter events, 0.0 us)
Async XLA Ops:
  313.8 4.6 %copy-start.1 = (bf16[8192,256]{1,0:T(8,128)(2,1)S(1)}, bf16[8192,256]{1,0:T(8,128)(2,1)}, u32[]{:S(2)}) copy-start(bf16[8192,256]{1,0:T(8,128)(2,1)} %get-tuple-element.7) | copy-start | bytes 12582916
  318.4 3.7 %copy-start = (bf16[2,64,16384]{2,1,0:T(8,128)(2,1)S(1)}, bf16[2,64,16384]{2,1,0:T(8,128)(2,1)}, u32[]{:S(2)}) copy-start(bf16[2,64,16384]{2,1,0:T(8,128)(2,1)} %get-tuple-element.14) | copy-start | bytes 12582916

commit v2 on v1

v2 whole, which is shorter than its diff:
```python
import jax
import jax.numpy as jnp
from jax import lax
from jax.experimental import pallas as pl
from jax.experimental.pallas import tpu as pltpu
from jax.sharding import PartitionSpec as P

BLOCK = 128
BY_MESH = pl.DeviceIdType.MESH

inner_rate = 0.25
outer_rate = 0.7
momentum_decay = 0.9

ISLANDS = 2
MEMBERS = 64
PEERS = ISLANDS * MEMBERS
CHIPS = PEERS // 2
ROWS = 64
OWN_TOKENS = 16
STRIDE = 91
CHIP_STRIDE = 29


def position():
    island = lax.axis_index("island")
    member = lax.axis_index("fsdp")
    return (member // 32) * 2 + island, (member // 8) % 4, (member // 2) % 4, member % 2


def member_of(y, z, x, core):
    return (y // 2) * 32 + z * 8 + x * 2 + core


def slot(far, sibling, near, half):
    return ((far * 2 + sibling) * 4 + near) * 2 + half


def cotangents(gate_pre, up_pre, upstream):
    logistic = jax.nn.sigmoid(gate_pre)
    d_gate = upstream * up_pre * logistic * (1.0 + gate_pre * (1.0 - logistic))
    d_up = upstream * gate_pre * logistic
    return d_gate.astype(jnp.bfloat16), d_up.astype(jnp.bfloat16)


def kernel(
    tokens_ref,
    hidden_ref,
    gate_ref,
    up_ref,
    momentum_ref,
    layout_ref,
    inverse_ref,
    gate_out,
    up_out,
    momentum_out,
    tokens,
    weights,
    hidden,
    cotangent,
    outgoing,
    gate_received,
    up_received,
    update,
    gate_sum,
    up_sum,
    load_sem,
    hidden_sem,
    tokens_sem,
    gather_sent,
    gather_got,
    sums_sent,
    sums_got,
    own_sem,
    updates_sent,
    updates_got,
    ready,
):
    received = (gate_received, up_received)
    y, z, x, core = position()
    island = lax.axis_index("island")
    member = lax.axis_index("fsdp")
    me = island * MEMBERS + member

    def partner(step):
        dy, dz, dx, dc = step // 32, (step // 8) % 4, (step // 2) % 4, step % 2
        there_y = (y + dy) % 4
        there = member_of(there_y, (z + dz) % 4, (x + dx) % 4, (core + dc) % 2)
        return there_y % 2, there

    near_plus, near_minus, far_plus, far_minus = (
        member_of(y, (z + dz) % 4, (x + dx) % 4, core)
        for dz, dx in (
            (core, 1 - core),
            (3 * core, 3 * (1 - core)),
            (1 - core, core),
            (3 * (1 - core), 3 * core),
        )
    )
    other_plane = member_of((y + 2) % 4, z, x, core)
    other_core = member_of(y, z, x, 1 - core)
    above, below = (y + 1) % 4, (y + 3) % 4
    barrier = pltpu.get_barrier_semaphore()
    greeted = [(island, near_plus), (island, near_minus), (island, far_plus), (island, far_minus)]
    greeted += [(island, other_plane), (island, other_core)]
    greeted += [(below % 2, member_of(below, z, x, core))]
    for there in greeted:
        pl.semaphore_signal(barrier, inc=1, device_id=there, device_id_type=BY_MESH)

    loads = [
        pltpu.make_async_copy(gate_ref, weights.at[0], load_sem.at[0]),
        pltpu.make_async_copy(up_ref, weights.at[1], load_sem.at[1]),
        pltpu.make_async_copy(momentum_ref, momentum_out, load_sem.at[2]),
    ]
    own_tokens = pltpu.make_async_copy(tokens_ref, tokens.at[0], tokens_sem)
    own_tokens.start()

    def load_hidden(place, carry):
        half, near, sibling, far = place % 2, (place // 2) % 4, (place // 8) % 2, place // 16
        their_core = (core + sibling) % 2
        dx = near * (1 - their_core) + far * their_core
        dz = near * their_core + far * (1 - their_core)
        there = member_of((y + 2 * half) % 4, (z + dz) % 4, (x + dx) % 4, their_core)
        rows = pl.ds(pl.multiple_of(there * OWN_TOKENS, OWN_TOKENS), OWN_TOKENS)
        pltpu.make_async_copy(hidden_ref.at[rows], hidden.at[place], hidden_sem).start()
        return carry

    lax.fori_loop(0, MEMBERS, load_hidden, 0)
    for load in loads:
        load.start()

    pl.semaphore_wait(barrier, len(greeted))

    def send_tokens(source, place, to):
        pltpu.make_async_remote_copy(
            src_ref=source,
            dst_ref=tokens.at[place],
            send_sem=gather_sent,
            recv_sem=gather_got.at[place],
            device_id=(island, to),
            device_id_type=BY_MESH,
        ).start()

    def arrived(place):
        pltpu.make_async_copy(tokens.at[place], tokens.at[place], gather_got.at[place]).wait()

    def spread(source, near, half):
        send_tokens(source, slot(3, 0, near, half), far_plus)
        send_tokens(source, slot(1, 0, near, half), far_minus)
        send_tokens(source, slot(0, 1, near, half), other_core)

    def ring(source, half):
        send_tokens(source, slot(0, 0, 3, half), near_plus)
        send_tokens(source, slot(0, 0, 1, half), near_minus)

    send_tokens(tokens_ref, slot(0, 0, 0, 1), other_plane)
    ring(tokens_ref, 0)
    spread(tokens_ref, 0, 0)

    place = slot(0, 0, 0, 1)
    arrived(place)
    ring(tokens.at[place], 1)
    spread(tokens.at[place], 0, 1)
    for half in range(2):
        before, after = slot(0, 0, 3, half), slot(0, 0, 1, half)
        arrived(before)
        if half == 0:
            send_tokens(tokens.at[before], slot(0, 0, 2, 0), near_plus)
        arrived(after)
        if half == 1:
            send_tokens(tokens.at[after], slot(0, 0, 2, 1), near_minus)
        spread(tokens.at[before], 3, half)
        spread(tokens.at[after], 1, half)
    for half in range(2):
        place = slot(0, 0, 2, half)
        arrived(place)
        spread(tokens.at[place], 2, half)

    def forward(far):
        depth = 1024
        for part in range(8):
            cols = pl.ds(part * depth, depth)
            rows = tokens[pl.ds(far * 16, 16), :, cols].reshape(256, depth)
            gate_part = jnp.dot(rows, weights[0, cols, :], preferred_element_type=jnp.float32)
            up_part = jnp.dot(rows, weights[1, cols, :], preferred_element_type=jnp.float32)
            if part == 0:
                gate_sum[...] = gate_part
                up_sum[...] = up_part
            else:
                gate_sum[...] += gate_part
                up_sum[...] += up_part
        upstream = hidden[pl.ds(far * 16, 16)].reshape(256, 256).astype(jnp.float32)
        d_gate, d_up = cotangents(gate_sum[...], up_sum[...], upstream)
        cotangent[pl.ds(far * 256, 256), 0:256] = d_gate
        cotangent[pl.ds(far * 256, 256), 256:512] = d_up

    own_tokens.wait()
    loads[0].wait()
    loads[1].wait()
    pltpu.make_async_copy(hidden, hidden, hidden_sem).wait()
    for near in range(4):
        for half in range(2):
            arrived(slot(0, 1, near, half))
    forward(0)

    order = [(0, 0), (0, 1), (1, 0), (3, 0), (1, 1), (3, 1), (2, 0), (2, 1)]
    for near, half in order:
        before, after = slot(3, 0, near, half), slot(1, 0, near, half)
        arrived(before)
        if half == 0:
            send_tokens(tokens.at[before], slot(2, 0, near, 0), far_plus)
        send_tokens(tokens.at[before], slot(3, 1, near, half), other_core)
        arrived(after)
        if half == 1:
            send_tokens(tokens.at[after], slot(2, 0, near, 1), far_minus)
        send_tokens(tokens.at[after], slot(1, 1, near, half), other_core)
    for far in (3, 1):
        for near, half in order:
            arrived(slot(far, 1, near, half))
        forward(far)
    for near, half in order:
        place = slot(2, 0, near, half)
        arrived(place)
        send_tokens(tokens.at[place], slot(2, 1, near, half), other_core)
    for near, half in order:
        arrived(slot(2, 1, near, half))
    pl.semaphore_signal(
        ready, inc=1, device_id=(above % 2, member_of(above, z, x, core)), device_id_type=BY_MESH
    )
    forward(2)
    pl.semaphore_wait(ready, 1)

    def send_sums(matrix, step):
        there_island, there = partner(step)
        number = there_island * MEMBERS + there

        @pl.when(number != me)
        def _():
            pltpu.make_async_remote_copy(
                src_ref=outgoing.at[matrix, pl.ds(number * 2, 2)],
                dst_ref=received[matrix].at[pl.ds(me * 2, 2)],
                send_sem=sums_sent,
                recv_sem=sums_got.at[matrix],
                device_id=(there_island, there),
                device_id_type=BY_MESH,
            ).start()

    def backward(matrix):
        def group_of_chips(group, carry):
            steps = [((group * 4 + k) * CHIP_STRIDE) % CHIPS for k in range(4)]
            chips = []
            for step in steps:
                there_island, there = partner(step * 2)
                chips.append(there_island * 32 + there // 2)
            columns = [
                tokens[:, :, pl.ds(pl.multiple_of(chip * BLOCK, BLOCK), BLOCK)].reshape(1024, BLOCK)
                for chip in chips
            ]
            summed = lax.dot_general(
                jnp.concatenate(columns, axis=1),
                cotangent[:, matrix * 256 : (matrix + 1) * 256],
                (((0,), (0,)), ((), ())),
                preferred_element_type=jnp.float32,
            )
            scaled = (inner_rate * summed).astype(jnp.bfloat16)
            for k in range(4):
                for half in range(2):
                    first = k * BLOCK + half * ROWS
                    for block in range(2):
                        outgoing[matrix, (chips[k] * 2 + half) * 2 + block] = scaled[
                            first : first + ROWS, block * BLOCK : (block + 1) * BLOCK
                        ]
            for k in range(4):
                send_sums(matrix, steps[k] * 2 + k % 2)
            return carry

        def other_cores(index, carry):
            send_sums(matrix, ((index * CHIP_STRIDE) % CHIPS) * 2 + (index + 1) % 2)
            return carry

        lax.fori_loop(0, CHIPS // 4, group_of_chips, 0)
        lax.fori_loop(0, CHIPS, other_cores, 0)
        received[matrix][pl.ds(me * 2, 2)] = outgoing[matrix, pl.ds(me * 2, 2)]

    backward(0)
    backward(1)
    loads[2].wait()

    mine = pl.ds(pl.multiple_of(me * ROWS, ROWS), ROWS)
    others = pl.ds(0, (PEERS - 1) * 2)
    all_others = [received[matrix].at[others] for matrix in range(2)]
    outs = (gate_out, up_out)

    def outer_step(matrix):
        def one_block(block, carry):
            first = inverse_ref[0, block]
            second = inverse_ref[1, block]
            cols = pl.ds(pl.multiple_of(block * BLOCK, BLOCK), BLOCK)
            one = received[matrix][first].astype(jnp.float32)
            two = received[matrix][second].astype(jnp.float32)
            average = (one + two) * (1.0 / ISLANDS)
            state = momentum_decay * momentum_out[matrix, :, cols].astype(jnp.float32) + average
            momentum_out[matrix, :, cols] = state.astype(jnp.bfloat16)
            update[matrix, block] = (outer_rate * (average + momentum_decay * state)).astype(
                jnp.bfloat16
            )
            return carry

        lax.fori_loop(0, PEERS, one_block, 0)

    def give_back(matrix):
        def stage(number, there_island, there):
            rows = pl.ds(pl.multiple_of(number * ROWS, ROWS), ROWS)
            for half in range(2):
                block = layout_ref[there_island, there * 2 + half]
                weights[matrix, rows, half * BLOCK : (half + 1) * BLOCK] = update[matrix, block]
            return rows

        def one_device(index, carry):
            there_island, there = partner((index * STRIDE) % PEERS)
            rows = stage(there_island * MEMBERS + there, there_island, there)
            pltpu.make_async_remote_copy(
                src_ref=weights.at[matrix, rows],
                dst_ref=outs[matrix].at[mine],
                send_sem=updates_sent,
                recv_sem=updates_got.at[matrix],
                device_id=(there_island, there),
                device_id_type=BY_MESH,
            ).start()
            return carry

        lax.fori_loop(1, PEERS, one_device, 0)
        stage(me, island, member)
        pltpu.make_async_copy(weights.at[matrix, mine], outs[matrix].at[mine], own_sem.at[matrix]).start()

    for matrix in range(2):
        pltpu.make_async_copy(all_others[matrix], all_others[matrix], sums_got.at[matrix]).wait()
        outer_step(matrix)
        give_back(matrix)

    sent = tokens.at[pl.ds(0, 63)]
    pltpu.make_async_copy(sent, sent, gather_sent).wait()
    for matrix in range(2):
        pltpu.make_async_copy(all_others[matrix], all_others[matrix], sums_sent).wait()
    for matrix in range(2):
        pltpu.make_async_copy(weights.at[matrix, mine], outs[matrix].at[mine], own_sem.at[matrix]).wait()
        part = outs[matrix].at[pl.ds(0, (PEERS - 1) * ROWS)]
        pltpu.make_async_copy(part, part, updates_got.at[matrix]).wait()
        pltpu.make_async_copy(part, part, updates_sent).wait()


def shards(tokens, hidden_grad, gate_weight, up_weight, momentum, layouts):
    blocks = layouts.shape[1]
    places = jnp.arange(blocks, dtype=jnp.int32)
    hit = layouts[:, :, None] == places[None, None, :]
    inverse = jnp.sum(jnp.where(hit, places[None, :, None], 0), axis=1, dtype=jnp.int32)
    inverse = inverse + jnp.arange(ISLANDS, dtype=jnp.int32)[:, None] * blocks
    anywhere = pl.BlockSpec(memory_space=pl.ANY)
    vmem = pl.BlockSpec(memory_space=pltpu.VMEM)
    scalars = pl.BlockSpec(memory_space=pltpu.SMEM)
    bf16 = jnp.bfloat16
    gate, up, state = pl.pallas_call(
        kernel,
        out_shape=(
            pltpu.VMEM((8192, 256), bf16),
            pltpu.VMEM((8192, 256), bf16),
            pltpu.VMEM((2, ROWS, 16384), bf16),
        ),
        in_specs=[anywhere] * 5 + [scalars] * 2,
        out_specs=(vmem, vmem, vmem),
        scratch_shapes=[
            pltpu.VMEM((MEMBERS, OWN_TOKENS, 8192), bf16),
            pltpu.VMEM((2, 8192, 256), bf16),
            pltpu.VMEM((MEMBERS, OWN_TOKENS, 256), bf16),
            pltpu.VMEM((1024, 512), bf16),
            pltpu.VMEM((2, PEERS * 2, ROWS, BLOCK), bf16),
            pltpu.VMEM((PEERS * 2, ROWS, BLOCK), bf16),
            pltpu.VMEM((PEERS * 2, ROWS, BLOCK), bf16),
            pltpu.VMEM((2, PEERS, ROWS, BLOCK), bf16),
            pltpu.VMEM((256, 256), jnp.float32),
            pltpu.VMEM((256, 256), jnp.float32),
            pltpu.SemaphoreType.DMA((3,)),
            pltpu.SemaphoreType.DMA,
            pltpu.SemaphoreType.DMA,
            pltpu.SemaphoreType.DMA,
            pltpu.SemaphoreType.DMA((64,)),
            pltpu.SemaphoreType.DMA,
            pltpu.SemaphoreType.DMA((2,)),
            pltpu.SemaphoreType.DMA((2,)),
            pltpu.SemaphoreType.DMA,
            pltpu.SemaphoreType.DMA((2,)),
            pltpu.SemaphoreType.REGULAR,
        ],
        compiler_params=pltpu.CompilerParams(
            collective_id=0, has_side_effects=True, vmem_limit_bytes=49 * 2**20
        ),
    )(tokens[0], hidden_grad[0], gate_weight[0], up_weight[0], momentum, layouts, inverse)
    return gate[None], up[None], state


def solution(mesh):
    placed = (
        P("island", "fsdp", None),
        P("island", None, "fsdp"),
        P("island", None, "fsdp"),
        P("island", None, "fsdp"),
        P(None, ("island", "fsdp"), None),
        P(),
    )
    return jax.shard_map(
        shards,
        mesh=mesh,
        in_specs=placed,
        out_specs=(
            P("island", None, "fsdp"),
            P("island", None, "fsdp"),
            P(None, ("island", "fsdp"), None),
        ),
        check_vma=False,
    )
```

time: 324 us -> 256 us (0.79)
  the two profiles are of different devices: /device:TPU:4 before, /device:TPU:7 now
where the time goes in v2:
time: 256 us
  Pallas kernels  248 us (97%)
  local copies, waits for them, and re-layouts  6.04 us (2%)
    pallas_call x1, Pallas kernels, shards(): pl.pallas_call(kernel, out_shape=(pltpu.VMEM((8192, 256), bf16), pltpu.VM...  248 us
    unnamed x3, local copies, waits for them, and re-layouts  6.04 us

profile of v2, /device:TPU:7, one launch (start us, length us, event | category | flops | bytes accessed | tf_op | source)
XLA Modules:
  0.0 255.9 jit_solution(3087482299150568589)
XLA Ops:
  0.6 0.8 select_reduce_fusion
  1.4 0.6 broadcast_add_fusion.inverse_ref
  2.1 247.8 %shard_map.85 = (bf16[8192,256]{1,0:T(8,128)(2,1)S(1)}, bf16[8192,256]{1,0:T(8,128)(2,1)S(1)}, bf16[2,64,16384]{2,1,0:T(8,128)(2,1)S(1)}) custom-call(bf16[16,8192]{1,0:T(8,128)(2,1)} %bitcast.11, bf16[1024,256]{1,0:T(8,128)(2,1)} %bitcast.10, bf16[8192,256]{1,0:T(8,128)(2,1)} %bitcast.8, bf16[8192,256]{1,0:T(8,128)(2,1)} %bitcast.9, ...), custom_call_target="tpu_custom_call" | custom-call | tf_op jit(solution)/shard_map/pallas_call | solution.py:362
  249.9 2.0 copy.12
  251.9 2.0 copy.13
  253.9 2.0 copy.14
  (1 shorter events, 0.0 us)

commit v3 on v2

--- a/solution.py
+++ b/solution.py
@@ -131,50 +131,62 @@
 
     pl.semaphore_wait(barrier, len(greeted))
 
-    def send_tokens(source, place, to):
+    def send_tokens(source, place, part, to):
+        cols = pl.ds(part * 4096, 4096)
         pltpu.make_async_remote_copy(
-            src_ref=source,
-            dst_ref=tokens.at[place],
+            src_ref=source.at[:, cols],
+            dst_ref=tokens.at[place, :, cols],
             send_sem=gather_sent,
-            recv_sem=gather_got.at[place],
+            recv_sem=gather_got.at[place * 2 + part],
             device_id=(island, to),
             device_id_type=BY_MESH,
         ).start()
 
-    def arrived(place):
-        pltpu.make_async_copy(tokens.at[place], tokens.at[place], gather_got.at[place]).wait()
-
-    def spread(source, near, half):
-        send_tokens(source, slot(3, 0, near, half), far_plus)
-        send_tokens(source, slot(1, 0, near, half), far_minus)
-        send_tokens(source, slot(0, 1, near, half), other_core)
-
-    def ring(source, half):
-        send_tokens(source, slot(0, 0, 3, half), near_plus)
-        send_tokens(source, slot(0, 0, 1, half), near_minus)
-
-    send_tokens(tokens_ref, slot(0, 0, 0, 1), other_plane)
-    ring(tokens_ref, 0)
-    spread(tokens_ref, 0, 0)
-
-    place = slot(0, 0, 0, 1)
-    arrived(place)
-    ring(tokens.at[place], 1)
-    spread(tokens.at[place], 0, 1)
-    for half in range(2):
-        before, after = slot(0, 0, 3, half), slot(0, 0, 1, half)
-        arrived(before)
-        if half == 0:
-            send_tokens(tokens.at[before], slot(0, 0, 2, 0), near_plus)
-        arrived(after)
-        if half == 1:
-            send_tokens(tokens.at[after], slot(0, 0, 2, 1), near_minus)
-        spread(tokens.at[before], 3, half)
-        spread(tokens.at[after], 1, half)
-    for half in range(2):
-        place = slot(0, 0, 2, half)
-        arrived(place)
-        spread(tokens.at[place], 2, half)
+    def arrived(place, part):
+        block = tokens.at[place, :, pl.ds(part * 4096, 4096)]
+        pltpu.make_async_copy(block, block, gather_got.at[place * 2 + part]).wait()
+
+    parts = range(2)
+
+    def spread(source, near, half, part):
+        send_tokens(source, slot(3, 0, near, half), part, far_plus)
+        send_tokens(source, slot(1, 0, near, half), part, far_minus)
+        send_tokens(source, slot(0, 1, near, half), part, other_core)
+
+    def ring(source, half, part):
+        send_tokens(source, slot(0, 0, 3, half), part, near_plus)
+        send_tokens(source, slot(0, 0, 1, half), part, near_minus)
+
+    for part in parts:
+        send_tokens(tokens_ref, slot(0, 0, 0, 1), part, other_plane)
+        ring(tokens_ref, 0, part)
+        spread(tokens_ref, 0, 0, part)
+
+    before, after = slot(0, 0, 3, 0), slot(0, 0, 1, 0)
+    for part in parts:
+        arrived(before, part)
+        send_tokens(tokens.at[before], slot(0, 0, 3, 1), part, other_plane)
+        if part % 2 == 0:
+            send_tokens(tokens.at[before], slot(0, 0, 2, 0), part, near_plus)
+        arrived(after, part)
+        send_tokens(tokens.at[after], slot(0, 0, 1, 1), part, other_plane)
+        if part % 2 == 1:
+            send_tokens(tokens.at[after], slot(0, 0, 2, 0), part, near_minus)
+        spread(tokens.at[before], 3, 0, part)
+        spread(tokens.at[after], 1, 0, part)
+    for part in parts:
+        arrived(slot(0, 0, 0, 1), part)
+        spread(tokens.at[slot(0, 0, 0, 1)], 0, 1, part)
+    place = slot(0, 0, 2, 0)
+    for part in parts:
+        arrived(place, part)
+        send_tokens(tokens.at[place], slot(0, 0, 2, 1), part, other_plane)
+        spread(tokens.at[place], 2, 0, part)
+    for near in (3, 1, 2):
+        place = slot(0, 0, near, 1)
+        for part in parts:
+            arrived(place, part)
+            spread(tokens.at[place], near, 1, part)
 
     def forward(far):
         depth = 1024
@@ -198,32 +210,35 @@
     loads[0].wait()
     loads[1].wait()
     pltpu.make_async_copy(hidden, hidden, hidden_sem).wait()
-    for near in range(4):
-        for half in range(2):
-            arrived(slot(0, 1, near, half))
+    def all_from_other_core(far):
+        for near in range(4):
+            for half in range(2):
+                for part in parts:
+                    arrived(slot(far, 1, near, half), part)
+
+    all_from_other_core(0)
     forward(0)
-
     order = [(0, 0), (0, 1), (1, 0), (3, 0), (1, 1), (3, 1), (2, 0), (2, 1)]
     for near, half in order:
         before, after = slot(3, 0, near, half), slot(1, 0, near, half)
-        arrived(before)
-        if half == 0:
-            send_tokens(tokens.at[before], slot(2, 0, near, 0), far_plus)
-        send_tokens(tokens.at[before], slot(3, 1, near, half), other_core)
-        arrived(after)
-        if half == 1:
-            send_tokens(tokens.at[after], slot(2, 0, near, 1), far_minus)
-        send_tokens(tokens.at[after], slot(1, 1, near, half), other_core)
+        for part in parts:
+            arrived(before, part)
+            if half == 0:
+                send_tokens(tokens.at[before], slot(2, 0, near, 0), part, far_plus)
+            send_tokens(tokens.at[before], slot(3, 1, near, half), part, other_core)
+            arrived(after, part)
+            if half == 1:
+                send_tokens(tokens.at[after], slot(2, 0, near, 1), part, far_minus)
+            send_tokens(tokens.at[after], slot(1, 1, near, half), part, other_core)
     for far in (3, 1):
-        for near, half in order:
-            arrived(slot(far, 1, near, half))
+        all_from_other_core(far)
         forward(far)
     for near, half in order:
         place = slot(2, 0, near, half)
-        arrived(place)
-        send_tokens(tokens.at[place], slot(2, 1, near, half), other_core)
-    for near, half in order:
-        arrived(slot(2, 1, near, half))
+        for part in parts:
+            arrived(place, part)
+            send_tokens(tokens.at[place], slot(2, 1, near, half), part, other_core)
+    all_from_other_core(2)
     pl.semaphore_signal(
         ready, inc=1, device_id=(above % 2, member_of(above, z, x, core)), device_id_type=BY_MESH
     )
@@ -353,8 +368,8 @@
     blocks = layouts.shape[1]
     places = jnp.arange(blocks, dtype=jnp.int32)
     hit = layouts[:, :, None] == places[None, None, :]
-    inverse = jnp.sum(jnp.where(hit, places[None, :, None], 0), axis=1, dtype=jnp.int32)
-    inverse = inverse + jnp.arange(ISLANDS, dtype=jnp.int32)[:, None] * blocks
+    lies = jnp.arange(ISLANDS * blocks, dtype=jnp.int32).reshape(ISLANDS, blocks)
+    inverse = jnp.sum(jnp.where(hit, lies[:, :, None], 0), axis=1, dtype=jnp.int32)
     anywhere = pl.BlockSpec(memory_space=pl.ANY)
     vmem = pl.BlockSpec(memory_space=pltpu.VMEM)
     scalars = pl.BlockSpec(memory_space=pltpu.SMEM)
@@ -383,7 +398,7 @@
             pltpu.SemaphoreType.DMA,
             pltpu.SemaphoreType.DMA,
             pltpu.SemaphoreType.DMA,
-            pltpu.SemaphoreType.DMA((64,)),
+            pltpu.SemaphoreType.DMA((128,)),
             pltpu.SemaphoreType.DMA,
             pltpu.SemaphoreType.DMA((2,)),
             pltpu.SemaphoreType.DMA((2,)),

time: 256 us -> 250 us (0.977)
  Pallas kernels: 248 us -> 239 us
    pallas_call x1, Pallas kernels: 248 us -> 239 us  [shards(): pl.pallas_call(kernel, out_shape=(pltpu.VMEM((8192, 256), bf16), pltpu.VM...]
where the time goes in v3:
time: 250 us; the launch traced here: 248 us
  Pallas kernels  239 us (96%)
  local copies, waits for them, and re-layouts  6.04 us (2%)
    pallas_call x1, Pallas kernels, shards(): pl.pallas_call(kernel, out_shape=(pltpu.VMEM((8192, 256), bf16), pltpu.VM...  239 us
    unnamed x3, local copies, waits for them, and re-layouts  6.04 us

profile of v3, /device:TPU:7, one launch (start us, length us, event | category | flops | bytes accessed | tf_op | source)
XLA Modules:
  0.0 247.6 jit_solution(4446730982177413145)
XLA Ops:
  0.6 1.4 select_reduce_fusion.inverse_ref
  2.0 239.5 %shard_map.85 = (bf16[8192,256]{1,0:T(8,128)(2,1)S(1)}, bf16[8192,256]{1,0:T(8,128)(2,1)S(1)}, bf16[2,64,16384]{2,1,0:T(8,128)(2,1)S(1)}) custom-call(bf16[16,8192]{1,0:T(8,128)(2,1)} %bitcast.11, bf16[1024,256]{1,0:T(8,128)(2,1)} %bitcast.10, bf16[8192,256]{1,0:T(8,128)(2,1)} %bitcast.8, bf16[8192,256]{1,0:T(8,128)(2,1)} %bitcast.9, ...), custom_call_target="tpu_custom_call" | custom-call | tf_op jit(solution)/shard_map/pallas_call | solution.py:377
  241.5 2.0 copy.12
  243.5 2.0 copy.13
  245.6 2.0 copy.14
  (1 shorter events, 0.0 us)

commit v4 on v3

--- a/solution.py
+++ b/solution.py
@@ -18,7 +18,7 @@
 CHIPS = PEERS // 2
 ROWS = 64
 OWN_TOKENS = 16
-STRIDE = 91
+STRIDE = 59
 CHIP_STRIDE = 29
 
 
@@ -83,7 +83,10 @@
     me = island * MEMBERS + member
 
     def partner(step):
-        dy, dz, dx, dc = step // 32, (step // 8) % 4, (step // 2) % 4, step % 2
+        first, second, third, dc = step // 32, (step // 8) % 4, (step // 2) % 4, step % 2
+        dy = first * (1 - core) + second * core
+        dz = second * (1 - core) + third * core
+        dx = third * (1 - core) + first * core
         there_y = (y + dy) % 4
         there = member_of(there_y, (z + dz) % 4, (x + dx) % 4, (core + dc) % 2)
         return there_y % 2, there

time: 250 us -> 249 us (level)
  no operation moved by 1% of the time
where the time goes in v4:
time: 249 us; the launch traced here: 247 us
  Pallas kernels  239 us (96%)
  local copies, waits for them, and re-layouts  6.04 us (2%)
    pallas_call x1, Pallas kernels, shards(): pl.pallas_call(kernel, out_shape=(pltpu.VMEM((8192, 256), bf16), pltpu.VM...  239 us
    unnamed x3, local copies, waits for them, and re-layouts  6.04 us

profile of v4, /device:TPU:7, one launch (start us, length us, event | category | flops | bytes accessed | tf_op | source)
XLA Modules:
  0.0 247.0 jit_solution(11484081844634958375)
XLA Ops:
  0.6 1.4 select_reduce_fusion.inverse_ref
  2.0 238.9 %shard_map.85 = (bf16[8192,256]{1,0:T(8,128)(2,1)S(1)}, bf16[8192,256]{1,0:T(8,128)(2,1)S(1)}, bf16[2,64,16384]{2,1,0:T(8,128)(2,1)S(1)}) custom-call(bf16[16,8192]{1,0:T(8,128)(2,1)} %bitcast.11, bf16[1024,256]{1,0:T(8,128)(2,1)} %bitcast.10, bf16[8192,256]{1,0:T(8,128)(2,1)} %bitcast.8, bf16[8192,256]{1,0:T(8,128)(2,1)} %bitcast.9, ...), custom_call_target="tpu_custom_call" | custom-call | tf_op jit(solution)/shard_map/pallas_call | solution.py:380
  240.9 2.0 copy.12
  242.9 2.0 copy.13
  245.0 2.0 copy.14
  (1 shorter events, 0.0 us)

commit v5 on v4

--- a/solution.py
+++ b/solution.py
@@ -118,20 +118,6 @@
     own_tokens = pltpu.make_async_copy(tokens_ref, tokens.at[0], tokens_sem)
     own_tokens.start()
 
-    def load_hidden(place, carry):
-        half, near, sibling, far = place % 2, (place // 2) % 4, (place // 8) % 2, place // 16
-        their_core = (core + sibling) % 2
-        dx = near * (1 - their_core) + far * their_core
-        dz = near * their_core + far * (1 - their_core)
-        there = member_of((y + 2 * half) % 4, (z + dz) % 4, (x + dx) % 4, their_core)
-        rows = pl.ds(pl.multiple_of(there * OWN_TOKENS, OWN_TOKENS), OWN_TOKENS)
-        pltpu.make_async_copy(hidden_ref.at[rows], hidden.at[place], hidden_sem).start()
-        return carry
-
-    lax.fori_loop(0, MEMBERS, load_hidden, 0)
-    for load in loads:
-        load.start()
-
     pl.semaphore_wait(barrier, len(greeted))
 
     def send_tokens(source, place, part, to):
@@ -164,6 +150,21 @@
         send_tokens(tokens_ref, slot(0, 0, 0, 1), part, other_plane)
         ring(tokens_ref, 0, part)
         spread(tokens_ref, 0, 0, part)
+
+    for load in loads:
+        load.start()
+
+    def load_hidden(place, carry):
+        half, near, sibling, far = place % 2, (place // 2) % 4, (place // 8) % 2, place // 16
+        their_core = (core + sibling) % 2
+        dx = near * (1 - their_core) + far * their_core
+        dz = near * their_core + far * (1 - their_core)
+        there = member_of((y + 2 * half) % 4, (z + dz) % 4, (x + dx) % 4, their_core)
+        rows = pl.ds(pl.multiple_of(there * OWN_TOKENS, OWN_TOKENS), OWN_TOKENS)
+        pltpu.make_async_copy(hidden_ref.at[rows], hidden.at[place], hidden_sem).start()
+        return carry
+
+    lax.fori_loop(0, MEMBERS, load_hidden, 0)
 
     before, after = slot(0, 0, 3, 0), slot(0, 0, 1, 0)
     for part in parts:

time: 249 us -> 268 us (1.076)
  Pallas kernels: 239 us -> 257 us
    pallas_call x1, Pallas kernels: 239 us -> 257 us  [shards(): pl.pallas_call(kernel, out_shape=(pltpu.VMEM((8192, 256), bf16), pltpu.VM...]
where the time goes in v5:
time: 268 us; the launch traced here: 265 us
  Pallas kernels  257 us (96%)
  local copies, waits for them, and re-layouts  6.04 us (2%)
    pallas_call x1, Pallas kernels, shards(): pl.pallas_call(kernel, out_shape=(pltpu.VMEM((8192, 256), bf16), pltpu.VM...  257 us
    unnamed x3, local copies, waits for them, and re-layouts  6.04 us

profile of v5, /device:TPU:7, one launch (start us, length us, event | category | flops | bytes accessed | tf_op | source)
XLA Modules:
  0.0 265.3 jit_solution(14356167419551064653)
XLA Ops:
  0.6 1.4 select_reduce_fusion.inverse_ref
  2.0 257.2 %shard_map.85 = (bf16[8192,256]{1,0:T(8,128)(2,1)S(1)}, bf16[8192,256]{1,0:T(8,128)(2,1)S(1)}, bf16[2,64,16384]{2,1,0:T(8,128)(2,1)S(1)}) custom-call(bf16[16,8192]{1,0:T(8,128)(2,1)} %bitcast.11, bf16[1024,256]{1,0:T(8,128)(2,1)} %bitcast.10, bf16[8192,256]{1,0:T(8,128)(2,1)} %bitcast.8, bf16[8192,256]{1,0:T(8,128)(2,1)} %bitcast.9, ...), custom_call_target="tpu_custom_call" | custom-call | tf_op jit(solution)/shard_map/pallas_call | solution.py:381
  259.3 2.0 copy.12
  261.3 2.0 copy.13
  263.3 2.0 copy.14
  (1 shorter events, 0.0 us)
